TPU v7x, 32 devices: a whole 2x2x4 slice. The times are simulated.
32 devices in a mesh: cases: 2 (over y), wheel: 4 (over z), inst: 4 (over x, core).
Axes of the slice: x: 2, y: 2, z: 4, core: 2. Of those that a mesh axis runs over, the one named last changes fastest.
Arguments:
- state: float32 [16, 5, 1024, 128], P('inst', None, ('cases', 'wheel')), parts along dimension 2, as said below
- slot_blade: int32 [8], P(('cases', 'wheel')), parts along dimension 0, may hold values from 0 to 3, each once
- blade_class: int32 [8], P('cases'), parts along dimension 0, may hold values from 0 to 3
- face_index: int32 [8, 2, 128], P(('cases', 'wheel')), parts along dimension 0, may hold values from 0 to 127, as said below
- class_amplitude: float32 [4], replicated, may hold values from 0.3 to 1.2
- class_phase: float32 [4], replicated, may hold values from -3.140625 to 3.140625
Outputs:
- new_state: float32 [16, 5, 1024, 128], P('inst', None, ('cases', 'wheel')), parts along dimension 2
- last_residual: float32 [16, 5, 1024, 128], P('inst', None, ('cases', 'wheel')), parts along dimension 2
There are 2 independent parts, one for each index of `cases`. A program takes and returns all parts, laid end to end along the dimension named above; an argument that names none is the same for every part. Nothing has to cross between parts.
Inputs may be any that keep to these rules, and one draw needn't show every extreme that they name: `state`: density lies in [0.8, 1.2] and pressure is positive in every cell. `slot_blade`: each blade sits in exactly one slot. face_index[s, side, k] differs from k by at most one.
All inputs are finite; a program needn't handle non-finite values.
Results may differ from a plain program's by a relative error of at most 0.0003.
Values sent between devices are 32-bit elements; how exact they have to be, the bound alone decides.
A program may use at most 64 MiB of HBM per device.

v0:
```python
import math

import jax
import jax.numpy as jnp
from jax import lax
from jax.sharding import PartitionSpec as P

INST = 16


HEAT_RATIO = 1.4
TIME_STEP = 0.05
DISSIPATION = 2.0
FREQUENCY = 0.5


def padded_2(shard, sides, width):
    for axis, dim in sides:
        size, length = (lax.axis_size(axis), shard.shape[dim])
        up = [(i, (i + 1) % size) for i in range(size)]
        down = [(j, i) for i, j in up]
        last = lax.slice_in_dim(shard, length - width, length, axis=dim)
        initial = lax.slice_in_dim(shard, 0, width, axis=dim)
        before = lax.ppermute(last, axis, up)
        after = lax.ppermute(initial, axis, down)
        shard = jnp.concatenate([before, shard, after], axis=dim)
    return shard


def fluxes(field):
    density = field[:, 0]
    axial_mom = field[:, 1]
    pitch_mom = field[:, 2]
    radial_mom = field[:, 3]
    energy = field[:, 4]
    inverse = 1.0 / density
    axial_vel = axial_mom * inverse
    pitch_vel = pitch_mom * inverse
    pressure = (HEAT_RATIO - 1.0) * (
        energy
        - 0.5 * (axial_mom * axial_mom + pitch_mom * pitch_mom + radial_mom * radial_mom) * inverse
    )
    enthalpy = energy + pressure
    axial_flux = jnp.stack(
        [
            axial_mom,
            axial_mom * axial_vel + pressure,
            pitch_mom * axial_vel,
            radial_mom * axial_vel,
            enthalpy * axial_vel,
        ],
        1,
    )
    pitch_flux = jnp.stack(
        [
            pitch_mom,
            axial_mom * pitch_vel,
            pitch_mom * pitch_vel + pressure,
            radial_mom * pitch_vel,
            enthalpy * pitch_vel,
        ],
        1,
    )
    return (axial_flux, pitch_flux)


def spectral_matrix(count):
    steps_apart = jnp.arange(count)[:, None] - jnp.arange(count)[None, :]
    apart = steps_apart != 0
    angle = jnp.where(apart, math.pi / count * steps_apart.astype(jnp.float32), 1.0)
    parity = jnp.where(steps_apart % 2 == 0, 1.0, -1.0)
    return jnp.where(apart, 0.5 * parity * jnp.cos(angle) / jnp.sin(angle), 0.0)


def face_terms(left, right, flux_left, flux_right, speed):
    return (
        0.5 * (flux_left + flux_right)
        - speed * 0.5 * (left + right)
        - 0.5 * DISSIPATION * (right - left)
    )


def local_residual(field, extended, speed, spectral):
    axial_ext, pitch_ext = fluxes(extended)
    axial_flux = axial_ext[:, :, 1:-1, :]
    axial_pad = jnp.concatenate([axial_flux[..., :1], axial_flux, axial_flux[..., -1:]], axis=3)
    field_pad = jnp.concatenate([field[..., :1], field, field[..., -1:]], axis=3)
    axial_face = face_terms(
        field_pad[..., :-1], field_pad[..., 1:], axial_pad[..., :-1], axial_pad[..., 1:], 0.0
    )
    pitch_face = face_terms(
        extended[:, :, :-1],
        extended[:, :, 1:],
        pitch_ext[:, :, :-1],
        pitch_ext[:, :, 1:],
        speed[:, None, None, None],
    )
    return (
        -(axial_face[..., 1:] - axial_face[..., :-1])
        - (pitch_face[:, :, 1:] - pitch_face[:, :, :-1])
        - FREQUENCY * spectral
    )


def body(state, slot_blade, blade_class, face_index, class_amplitude, class_phase):
    per_dev = state.shape[0]
    own_start = lax.axis_index("inst") * per_dev
    blade = slot_blade[0]
    class_id = jnp.sum(jnp.where(jnp.arange(blade_class.shape[0]) == blade, blade_class, 0))
    class_pick = jnp.arange(class_amplitude.shape[0]) == class_id
    amplitude = jnp.sum(jnp.where(class_pick, class_amplitude, 0.0))
    phase = jnp.sum(jnp.where(class_pick, class_phase, 0.0))
    matrix = spectral_matrix(INST)
    face_row = face_index[0]
    instance = (own_start + jnp.arange(per_dev)).astype(jnp.float32)
    speed = amplitude * jnp.sin(2.0 * math.pi / INST * instance + phase)
    own_rows = lax.dynamic_slice_in_dim(matrix, own_start, per_dev, 0)

    def spectral_of(field):
        return jnp.einsum(
            "nm,mvjk->nvjk",
            own_rows,
            lax.all_gather(field, "inst", axis=0, tiled=True),
            precision=lax.Precision.HIGHEST,
        )

    def residual_of(field):
        padded = padded_2(field, (("wheel", 2),), 1)
        lower = jnp.take(padded[:, :, 0, :], face_row[0], axis=2)
        upper = jnp.take(padded[:, :, -1, :], face_row[1], axis=2)
        extended = jnp.concatenate([lower[:, :, None, :], field, upper[:, :, None, :]], axis=2)
        return local_residual(field, extended, speed, spectral_of(field))

    first = state + 0.5 * TIME_STEP * residual_of(state)
    last_residual = residual_of(first)
    new_state = state + TIME_STEP * last_residual
    return (new_state, last_residual)


def solution(mesh):
    placed = (
        P("inst", None, ("cases", "wheel"), None),
        P(("cases", "wheel")),
        P("cases"),
        P(("cases", "wheel"), None, None),
        P(),
        P(),
    )
    return jax.shard_map(
        body,
        mesh=mesh,
        in_specs=placed,
        out_specs=(
            P("inst", None, ("cases", "wheel"), None),
            P("inst", None, ("cases", "wheel"), None),
        ),
        check_vma=False,
    )
```

profile of v0, /device:TPU:0, one launch (start us, length us, event | category | flops | bytes accessed | tf_op | source)
XLA Modules:
  0.0 127.6 jit_solution(13102067222919137972)
XLA Ops:
  7.2 0.0 all-gather.3.cloned.1.call-start
  7.2 0.7 all-gather.3.cloned.1.call-update
  7.9 0.0 all-gather.5.cloned.1.call-start
  8.0 0.9 fusion.54
  8.9 0.0 copy-start.6
  8.9 0.0 copy-start.7
  8.9 0.0 copy-start.8
  8.9 3.1 %collective-permute-start = (f32[4,5,1,128]{3,2,1,0:T(1,128)S(1)}, f32[4,5,1,128]{3,2,1,0:T(1,128)S(1)}, u32[]{:S(2)}, u32[]{:S(2)}) collective-permute-start(f32[4,5,1,128]{3,2,1,0:T(1,128)S(1)} %get-tuple-element.43), channel_id=1, source_target_pairs={{0,4},{4,8},{8,12},{12,0},{1,5},{5,9},{9,13},{13,1},{2,6},{6,10},{... | collective-permute-start | bytes 30728 | tf_op jit(solution)/shard_map/ppermute | solution.py:24
  12.0 2.1 %collective-permute-start.1 = (f32[4,5,1,128]{3,2,1,0:T(1,128)S(1)}, f32[4,5,1,128]{3,2,1,0:T(1,128)S(1)}, u32[]{:S(2)}, u32[]{:S(2)}) collective-permute-start(f32[4,5,1,128]{3,2,1,0:T(1,128)S(1)} %get-tuple-element.44), channel_id=1, source_target_pairs={{4,0},{8,4},{12,8},{0,12},{5,1},{9,5},{13,9},{1,13},{6,2},{10,6},{... | collective-permute-start | bytes 30728 | tf_op jit(solution)/shard_map/ppermute | solution.py:25
  14.1 0.8 copy.63
  15.7 0.6 fusion.46
  16.3 1.3 %fusion.44 = f32[]{:T(128)} fusion(f32[4]{0:T(128)S(1)} %copy-done.7, s32[]{:T(128)} %fusion.46), kind=kLoop, calls=%fused_computation.106 | loop fusion | flops 11 | bytes 24 | tf_op jit(solution)/shard_map/reduce_sum | solution.py:111
  17.6 1.3 fusion.45
  18.9 2.2 %fusion.53 = (f32[4,5,128,1]{3,0,2,1:T(4,128)}, f32[4,5,128,1]{3,0,2,1:T(4,128)}) fusion(f32[4,5,128,128]{3,0,2,1:T(4,128)S(1)} %copy.63), kind=kLoop, calls=%fused_computation.114 | loop fusion | bytes 40960 | tf_op jit(solution)/shard_map/slice | solution.py:87
  21.2 1.3 %multiply_multiply_fusion = f32[4]{0:T(128)S(1)} fusion(f32[]{:T(128)} %fusion.45, s32[]{:T(128)S(6)} %mul.290, f32[]{:T(128)} %fusion.44), kind=kLoop, calls=%fused_computation.109 | loop fusion | flops 24 | bytes 28 | tf_op jit(solution)/shard_map/mul | solution.py:78
  22.5 0.2 copy.67
  22.7 0.8 gather_fusion
  23.5 0.1 copy.44
  23.6 0.2 copy.68
  23.8 0.8 gather_fusion.1
  24.5 0.1 copy.47
  24.7 0.3 pad_maximum_fusion.4
  25.0 0.3 add_dynamic-update-slice_fusion.3
  25.3 0.1 multiply_dynamic-update-slice_fusion.11
  25.4 0.2 multiply_dynamic-update-slice_fusion.8
  25.6 0.2 multiply_dynamic-update-slice_fusion.9
  25.9 0.1 slice.198
  26.0 0.1 multiply_dynamic-update-slice_fusion.7
  26.1 0.1 multiply_dynamic-update-slice_fusion.6
  26.2 0.7 fusion.50
  26.9 0.0 copy-start.1
  27.0 0.0 copy-start.2
  27.0 1.9 %fusion.30 = f32[4,5,129,128]{3,0,2,1:T(4,128)} fusion(f32[4,5,130,128]{3,0,2,1:T(4,128)S(1)} %multiply_dynamic-update-slice_fusion.6, f32[4,5,1,128]{3,0,2,1:T(4,128)S(1)} %select_bitcast_fusion.2, f32[4,5,128,128]{3,0,2,1:T(4,128)S(1)} %copy.63, f32[4,5,1,128]{3,0,2,1:T(4,128)S(1)} %select_bitcast_fusion.3, f32[4]{0:T(128)S(1)} %multiply_multiply_fusion), kind=kLoop, calls=%fused_computation.34 | loop fusion | flops 2972160 | bytes 5294096 | tf_op jit(solution)/shard_map/sub | solution.py:77
  28.9 0.1 copy-done.2
  28.9 4.3 %fusion.6 = f32[4,5,128,129]{3,0,2,1:T(4,128)} fusion(f32[4,5,128,128]{3,0,2,1:T(4,128)S(1)} %slice.198, f32[4,5,128,1]{3,0,2,1:T(4,128)S(1)} %get-tuple-element.33, f32[4,5,128,1]{3,0,2,1:T(4,128)S(1)} %get-tuple-element.32, f32[4,5,128,1]{3,0,2,1:T(4,128)S(1)} %copy-done.2, f32[4,5,128,128]{3,0,2,1:T(4,128)S(1)} %copy.63, f32[4,5,128,1]{3,0,2,1:T(4,128)S(1)} %copy-done.1), kind=kLoop, calls=%fused_computation.11 | loop fusion | flops 3632640 | bytes 3983360 | tf_op jit(solution)/shard_map/sub | solution.py:77
  33.3 19.5 %all-gather.3.cloned.1.call-done = f32[16,5,128,128]{3,2,1,0:T(8,128)} async-done(((f32[4,5,128,128]{3,2,1,0:T(8,128)}), f32[16,5,128,128]{3,2,1,0:T(8,128)}) %all-gather.3.cloned.1.call-update) | async-done | bytes 5242896 | tf_op jit(solution)/shard_map/all_gather | solution.py:123
  52.7 11.8 %fusion.35 = f32[4,5,128,128]{3,0,2,1:T(4,128)S(1)} fusion(f32[16,5,128,128]{3,2,1,0:T(8,128)} %all-gather.3.cloned.1.call-done, f32[4,5,129,128]{3,0,2,1:T(4,128)} %fusion.30, f32[4,5,128,129]{3,0,2,1:T(4,128)} %fusion.6, f32[16,16]{1,0:T(8,128)S(1)} %fusion.39, s32[]{:T(128)S(6)} %select_n.46, s32[16,16]{1,0:T(8,128)S(1)} %iota_subtract_fusion, ...), kind=kOutput, calls=%fused_computation.47 | convolution fusion | flops 65536576 | bytes 13113348 | tf_op jit(solution)/shard_map/nm,mvjk->nvjk/dot_general | solution.py:120
  64.6 1.2 copy.61
  65.8 0.0 all-gather.5.cloned.1.call-update
  65.8 1.5 %collective-permute-start.2 = (f32[4,5,1,128]{3,0,2,1:T(4,128)S(1)}, f32[4,5,1,128]{3,0,2,1:T(4,128)S(1)}, u32[]{:S(2)}, u32[]{:S(2)}) collective-permute-start(f32[4,5,1,128]{3,0,2,1:T(4,128)S(1)} %get-tuple-element.39), channel_id=1, source_target_pairs={{0,4},{4,8},{8,12},{12,0},{1,5},{5,9},{9,13},{13,1},{2,6},{6,10},{... | collective-permute-start | bytes 30728 | tf_op jit(solution)/shard_map/ppermute | solution.py:24
  67.3 2.3 %collective-permute-start.3 = (f32[4,5,1,128]{3,0,2,1:T(4,128)S(1)}, f32[4,5,1,128]{3,0,2,1:T(4,128)S(1)}, u32[]{:S(2)}, u32[]{:S(2)}) collective-permute-start(f32[4,5,1,128]{3,0,2,1:T(4,128)S(1)} %get-tuple-element.40), channel_id=1, source_target_pairs={{4,0},{8,4},{12,8},{0,12},{5,1},{9,5},{13,9},{1,13},{6,2},{10,6},{... | collective-permute-start | bytes 30728 | tf_op jit(solution)/shard_map/ppermute | solution.py:25
  69.7 2.3 %fusion.51 = (f32[4,5,128,1]{3,0,2,1:T(4,128)}, f32[4,5,128,1]{3,0,2,1:T(4,128)}) fusion(f32[4,5,128,128]{3,0,2,1:T(4,128)S(1)} %fusion.35), kind=kLoop, calls=%fused_computation.112 | loop fusion | bytes 40960 | tf_op jit(solution)/shard_map/slice | solution.py:87
  72.0 0.2 copy.57
  72.1 0.8 gather_fusion.2
  72.9 0.1 copy.58
  73.0 0.2 copy.59
  73.2 0.8 gather_fusion.3
  74.0 0.1 copy.60
  74.1 0.3 pad_maximum_fusion.5
  74.4 0.3 add_dynamic-update-slice_fusion.1
  74.7 0.1 multiply_dynamic-update-slice_fusion.5
  74.8 0.2 multiply_dynamic-update-slice_fusion.2
  75.1 0.2 multiply_dynamic-update-slice_fusion.3
  75.3 0.1 slice.216
  75.4 0.1 multiply_dynamic-update-slice_fusion.1
  75.5 0.1 multiply_dynamic-update-slice_fusion
  75.6 0.7 fusion.49
  76.4 0.0 copy-start.3
  76.4 1.9 %fusion.27 = f32[4,5,129,128]{3,0,2,1:T(4,128)} fusion(f32[4,5,130,128]{3,0,2,1:T(4,128)S(1)} %multiply_dynamic-update-slice_fusion, f32[4,5,1,128]{3,0,2,1:T(4,128)S(1)} %get-tuple-element.49, f32[4,5,128,128]{3,0,2,1:T(4,128)S(1)} %fusion.35, f32[4,5,1,128]{3,0,2,1:T(4,128)S(1)} %get-tuple-element.50, f32[4]{0:T(128)S(1)} %multiply_multiply_fusion), kind=kLoop, calls=%fused_computation.30 | loop fusion | flops 2972160 | bytes 5294096 | tf_op jit(solution)/shard_map/sub | solution.py:77
  78.3 4.3 %fusion.9 = f32[4,5,128,129]{3,0,2,1:T(4,128)} fusion(f32[4,5,128,128]{3,0,2,1:T(4,128)S(1)} %slice.216, f32[4,5,128,1]{3,0,2,1:T(4,128)S(1)} %get-tuple-element.28, f32[4,5,128,1]{3,0,2,1:T(4,128)S(1)} %get-tuple-element.27, f32[4,5,128,1]{3,0,2,1:T(4,128)S(1)} %copy-done.4, f32[4,5,128,128]{3,0,2,1:T(4,128)S(1)} %fusion.35, f32[4,5,128,1]{3,0,2,1:T(4,128)S(1)} %copy-done.3), kind=kLoop, calls=%fused_computation.17 | loop fusion | flops 3632640 | bytes 3983360 | tf_op jit(solution)/shard_map/sub | solution.py:77
  82.6 23.8 %all-gather.5.cloned.1.call-done = f32[16,5,128,128]{3,2,1,0:T(8,128)} async-done(((f32[4,5,128,128]{3,2,1,0:T(8,128)}), f32[16,5,128,128]{3,2,1,0:T(8,128)}) %all-gather.5.cloned.1.call-update) | async-done | bytes 5242896 | tf_op jit(solution)/shard_map/all_gather | solution.py:123
  106.4 11.9 %multiply_add_fusion = (f32[4,5,128,128]{3,0,2,1:T(4,128)S(1)}, f32[4,5,128,128]{3,0,2,1:T(4,128)S(1)}) fusion(f32[4,5,128,128]{3,2,1,0:T(8,128)S(1)} %copy-done, f32[16,5,128,128]{3,2,1,0:T(8,128)} %all-gather.5.cloned.1.call-done, f32[16,16]{1,0:T(8,128)S(1)} %fusion.39, s32[]{:T(128)S(6)} %select_n.46, s32[16,16]{1,0:T(8,128)S(1)} %add_select_fusion, ...), kind=kOutput, calls=%fused_computation.48 | convolution fusion | flops 65536576 | bytes 14424068 | tf_op jit(solution)/shard_map/nm,mvjk->nvjk/dot_general | solution.py:120
  118.3 1.2 copy.64
  119.5 1.2 copy.65
  (27 shorter events, 0.2 us)
Async XLA Ops:
  7.2 7.0 %copy-start = (f32[4,5,128,128]{3,2,1,0:T(8,128)S(1)}, f32[4,5,128,128]{3,2,1,0:T(8,128)}, u32[]{:S(2)}) copy-start(f32[4,5,128,128]{3,2,1,0:T(8,128)} %param.8) | copy-start | bytes 3932164
  7.2 45.6 %all-gather.3.cloned.1.call-start = ((), (), s32[]{:S(2)}) async-start(), calls=%async_computation | async-start | bytes 6553600 | tf_op jit(solution)/shard_map/all_gather | solution.py:123
  7.9 7.7 %copy-start.5 = (s32[1,2,128]{2,1,0:T(2,128)S(1)}, s32[1,2,128]{2,1,0:T(2,128)}, u32[]{:S(2)}) copy-start(s32[1,2,128]{2,1,0:T(2,128)} %param.11) | copy-start | bytes 3076
  7.9 98.5 %all-gather.5.cloned.1.call-start = ((), (), s32[]{:S(2)}) async-start(), calls=%async_computation.1 | async-start | bytes 6553600 | tf_op jit(solution)/shard_map/all_gather | solution.py:123
  8.9 6.8 %copy-start.6 = (s32[4]{0:T(128)S(1)}, s32[4]{0:T(128)}, u32[]{:S(2)}) copy-start(s32[4]{0:T(128)} %param.10) | copy-start | bytes 52
  8.9 7.4 %copy-start.7 = (f32[4]{0:T(128)S(1)}, f32[4]{0:T(128)}, u32[]{:S(2)}) copy-start(f32[4]{0:T(128)} %param.12) | copy-start | bytes 52
  8.9 8.7 %copy-start.8 = (f32[4]{0:T(128)S(1)}, f32[4]{0:T(128)}, u32[]{:S(2)}) copy-start(f32[4]{0:T(128)} %param.13) | copy-start | bytes 52
  8.9 13.6 %collective-permute-start = (f32[4,5,1,128]{3,2,1,0:T(1,128)S(1)}, f32[4,5,1,128]{3,2,1,0:T(1,128)S(1)}, u32[]{:S(2)}, u32[]{:S(2)}) collective-permute-start(f32[4,5,1,128]{3,2,1,0:T(1,128)S(1)} %get-tuple-element.43), channel_id=1, source_target_pairs={{0,4},{4,8},{8,12},{12,0},{1,5},{5,9},{9,13},{13,1},{2,6},{6,10},{... | collective-permute-start | bytes 30728 | tf_op jit(solution)/shard_map/ppermute | solution.py:24
  12.0 11.5 %collective-permute-start.1 = (f32[4,5,1,128]{3,2,1,0:T(1,128)S(1)}, f32[4,5,1,128]{3,2,1,0:T(1,128)S(1)}, u32[]{:S(2)}, u32[]{:S(2)}) collective-permute-start(f32[4,5,1,128]{3,2,1,0:T(1,128)S(1)} %get-tuple-element.44), channel_id=1, source_target_pairs={{4,0},{8,4},{12,8},{0,12},{5,1},{9,5},{13,9},{1,13},{6,2},{10,6},{... | collective-permute-start | bytes 30728 | tf_op jit(solution)/shard_map/ppermute | solution.py:25
  26.9 1.9 %copy-start.1 = (f32[4,5,128,1]{3,0,2,1:T(4,128)S(1)}, f32[4,5,128,1]{3,0,2,1:T(4,128)}, u32[]{:S(2)}) copy-start(f32[4,5,128,1]{3,0,2,1:T(4,128)} %get-tuple-element.41) | copy-start | bytes 30724
  27.0 2.0 %copy-start.2 = (f32[4,5,128,1]{3,0,2,1:T(4,128)S(1)}, f32[4,5,128,1]{3,0,2,1:T(4,128)}, u32[]{:S(2)}) copy-start(f32[4,5,128,1]{3,0,2,1:T(4,128)} %get-tuple-element.42) | copy-start | bytes 30724
  65.8 6.1 %collective-permute-start.2 = (f32[4,5,1,128]{3,0,2,1:T(4,128)S(1)}, f32[4,5,1,128]{3,0,2,1:T(4,128)S(1)}, u32[]{:S(2)}, u32[]{:S(2)}) collective-permute-start(f32[4,5,1,128]{3,0,2,1:T(4,128)S(1)} %get-tuple-element.39), channel_id=1, source_target_pairs={{0,4},{4,8},{8,12},{12,0},{1,5},{5,9},{9,13},{13,1},{2,6},{6,10},{... | collective-permute-start | bytes 30728 | tf_op jit(solution)/shard_map/ppermute | solution.py:24
  67.3 5.6 %collective-permute-start.3 = (f32[4,5,1,128]{3,0,2,1:T(4,128)S(1)}, f32[4,5,1,128]{3,0,2,1:T(4,128)S(1)}, u32[]{:S(2)}, u32[]{:S(2)}) collective-permute-start(f32[4,5,1,128]{3,0,2,1:T(4,128)S(1)} %get-tuple-element.40), channel_id=1, source_target_pairs={{4,0},{8,4},{12,8},{0,12},{5,1},{9,5},{13,9},{1,13},{6,2},{10,6},{... | collective-permute-start | bytes 30728 | tf_op jit(solution)/shard_map/ppermute | solution.py:25
  76.4 1.9 %copy-start.3 = (f32[4,5,128,1]{3,0,2,1:T(4,128)S(1)}, f32[4,5,128,1]{3,0,2,1:T(4,128)}, u32[]{:S(2)}) copy-start(f32[4,5,128,1]{3,0,2,1:T(4,128)} %get-tuple-element.37) | copy-start | bytes 30724
  76.4 1.9 %copy-start.4 = (f32[4,5,128,1]{3,0,2,1:T(4,128)S(1)}, f32[4,5,128,1]{3,0,2,1:T(4,128)}, u32[]{:S(2)}) copy-start(f32[4,5,128,1]{3,0,2,1:T(4,128)} %get-tuple-element.38) | copy-start | bytes 30724
Sparse Core Ops, SparseCore 0:
  9.6 43.1 all-gather.2
  65.9 40.4 all-gather.4
where the time goes:
time: 128 us
  waiting for transfers between devices  43.9 us (34%)
  matrix products  23.7 us (19%)
  other arithmetic  19.8 us (15%)
  local copies, waits for them, and re-layouts  15.9 us (12%)
  between operations  15.1 us (12%)
  starting transfers between devices  9.12 us (7%)
    all_gather x2, waiting for transfers between devices, spectral_of(): lax.all_gather(field, 'inst', axis=0, tiled=True)  43.2 us
    dot_general x2, matrix products, spectral_of(): jnp.einsum('nm,mvjk->nvjk', own_rows, lax.all_gather(field, 'inst', axis=...  23.7 us
    sub x4, other arithmetic, face_terms(): 0.5 * (flux_left + flux_right) - speed * 0.5 * (left + right)  12.4 us
    ppermute x2, starting transfers between devices, padded_2(): before = lax.ppermute(last, axis, up)  4.62 us
    slice x2, local copies, waits for them, and re-layouts, local_residual(): field[..., :1]  4.51 us
    ppermute x2, starting transfers between devices, padded_2(): after = lax.ppermute(initial, axis, down)  4.43 us
    unnamed x23, local copies, waits for them, and re-layouts  3.41 us
  transfers between devices with their start and end apart: 6, of which 2 were waited for; matrix products, arithmetic and copies ran while one was open for 25% of the time, Pallas kernels for 0%

commit v1 on v0

v1 whole, which is shorter than its diff:
```python
import functools
import math

import jax
import jax.numpy as jnp
from jax import lax
from jax.experimental import pallas as pl
from jax.experimental.pallas import tpu as pltpu
from jax.sharding import PartitionSpec as P

TIME_STEP = 0.05
GAMMA1 = 0.4
FREQUENCY = 0.5
NV = 5
MESH = pl.DeviceIdType.MESH


def flip(i, off):
    out, b = i, 1
    while b <= off:
        if off & b:
            out = out + b - 2 * b * ((i // b) % 2)
        b *= 2
    return out


def spectral(q):
    s = [q[i] + q[i + 8] for i in range(8)]
    d = [q[i] - q[i + 8] for i in range(8)]
    c = [0.5 * (-1) ** k / math.tan(math.pi * k / 8) for k in range(1, 4)]
    t = [0.5 * (-1) ** k / math.sin(math.pi * k / 8) for k in range(1, 4)]
    s2 = [s[i] - s[(i + 2) % 8] for i in range(8)]
    s4 = [s[i] - s[i + 4] for i in range(4)]

    def dd(i):
        i %= 16
        return (d[i], 1) if i < 8 else (d[i - 8], -1)

    cache = {}

    def ddiff(i, j):
        (x, sx), (y, sy) = dd(i), dd(j)
        key = (i % 8, j % 8, sx * sy)
        if key not in cache:
            cache[key] = x - y if sx * sy > 0 else x + y
        return cache[key], sx

    out = [None] * 16
    for n in range(8):
        a1 = s2[(n - 1) % 8]
        a3 = s2[(n + 3) % 8]
        i = (n - 2) % 8
        a2 = s4[i] * c[1] if i < 4 else s4[i - 4] * (-c[1])
        u = c[0] * a1 - c[2] * a3 + a2
        w = None
        for k in (1, 2, 3):
            v, sg = ddiff(n - k, n + k)
            term = v * (sg * t[k - 1])
            w = term if w is None else w + term
        x, sg = dd(n - 4)
        w = w + x * (0.5 * sg)
        out[n] = u + w
        out[n + 8] = u - w
    return out


def shift(x, k, axis):
    size = x.shape[axis]
    return pltpu.roll(x, k % size, axis)


def kernel(n_i, n_w, per, rows, state, slot_blade, blade_class, amp, phase, face, res,
           qx, fx, rs, spd, own_sem, snd_m, rcv_m, snd_h, rcv_h, snd_f, rcv_f, snd_r, rcv_r):
    me = lax.axis_index("inst")
    w = lax.axis_index("wheel")
    up_w, dn_w = lax.rem(w + 1, n_w), lax.rem(w + n_w - 1, n_w)
    ct = rows * n_i
    inst = n_i * per
    ext = rows + 8

    def dev(wheel, i):
        return {"wheel": wheel, "inst": i}

    barrier = pltpu.get_barrier_semaphore()
    for off in range(1, n_i):
        pl.semaphore_signal(barrier, inc=1, device_id=dev(w, flip(me, off)), device_id_type=MESH)

    @pl.when(me == 0)
    def _():
        for j in range(n_i):
            pl.semaphore_signal(barrier, inc=1, device_id=dev(dn_w, j), device_id_type=MESH)

    @pl.when(me == n_i - 1)
    def _():
        for j in range(n_i):
            pl.semaphore_signal(barrier, inc=1, device_id=dev(up_w, j), device_id_type=MESH)

    mine = pl.ds(me * per, per)
    own_copy = pltpu.make_async_copy(
        state.at[:, :, pl.ds(me * rows, rows), :], qx.at[mine, :, pl.ds(0, rows), :], own_sem.at[0])
    own_copy.start()
    cls = blade_class[slot_blade[0]]
    instance = lax.broadcasted_iota(jnp.int32, (inst, 128), 0).astype(jnp.float32)
    spd[...] = amp[cls] * jnp.sin((2.0 * math.pi / inst) * instance + phase[cls])
    lane = lax.broadcasted_iota(jnp.int32, (8, 128), 1)
    sub = lax.broadcasted_iota(jnp.int32, (8, 128), 0)
    lo_idx = jnp.where(me == 0, face[0, 0:1, :], lane[0:1])
    hi_idx = jnp.where(me == n_i - 1, face[0, 1:2, :], lane[0:1])
    offs = jnp.where(sub == 0, hi_idx, jnp.where(sub == 7, lo_idx, lane)) - lane

    pl.semaphore_wait(barrier, n_i + 1)

    def halo(side, i):
        if side == 0:
            row, slot, wheel = (rows * i - 1) % ct, ext - 1, (up_w if i == 0 else w)
            far = i == 0
        else:
            row, slot, wheel = (rows * (i + 1)) % ct, rows, (dn_w if i == n_i - 1 else w)
            far = i == n_i - 1
        src = state.at[:, :, pl.ds(row, 1), :]
        dst = qx.at[mine, :, pl.ds(slot, 1), :]
        remote = pltpu.make_async_remote_copy(
            src, dst, snd_h.at[side, i], rcv_h.at[side, me], device_id=dev(wheel, i), device_id_type=MESH)
        local = pltpu.make_async_copy(src, dst, rcv_h.at[side, me])
        return far, remote, local

    for side in range(2):
        for i in range(n_i):
            far, remote, local = halo(side, i)
            if far:
                remote.start()
            else:
                @pl.when(me != i)
                def _(remote=remote):
                    remote.start()

                @pl.when(me == i)
                def _(local=local):
                    local.start()

    def main(off):
        to = flip(me, off)
        return pltpu.make_async_remote_copy(
            state.at[:, :, pl.ds(to * rows, rows), :], qx.at[mine, :, pl.ds(0, rows), :],
            snd_m.at[off], rcv_m.at[off], device_id=dev(w, to), device_id_type=MESH)

    order_out = list(range(2, n_i)) + [1]
    for off in order_out:
        main(off).start()

    first_lane = lax.broadcasted_iota(jnp.int32, (rows, 128), 1) == 0
    last_lane = lax.broadcasted_iota(jnp.int32, (rows, 128), 1) == 127

    def flux_part(buf, n):
        halo_q = []
        for v in range(NV):
            x = buf[n, v, pl.ds(rows, 8), :]
            halo_q.append(jnp.where(offs == 0, x, jnp.where(offs == 1, shift(x, -1, 1), shift(x, 1, 1))))
        q = [jnp.concatenate([buf[n, v, pl.ds(0, rows), :], halo_q[v]], axis=0) for v in range(NV)]
        rho, mx, mt, mr, en = q
        inv = 1.0 / rho
        ux, ut = mx * inv, mt * inv
        p = GAMMA1 * (en - 0.5 * (mx * ux + mt * ut + mr * mr * inv))
        h = en + p
        speed = spd[pl.ds(n, 1), :]
        hux = 0.5 * ux[:rows]
        hut = 0.5 * ut
        hrel = hut - 0.5 * speed
        hp = 0.5 * p
        out = []
        for v in range(NV):
            base = h if v == 4 else q[v]
            g = base[:rows] * hux
            f = q[v] * hrel
            if v == 1:
                g = g + hp[:rows]
            if v == 2:
                f = f + hp
            if v == 4:
                f = f + p * hut
            qc = q[v][:rows]
            a_ax, b_ax = g - qc, g + qc
            right = jnp.where(last_lane, a_ax, shift(a_ax, -1, 1))
            left = jnp.where(first_lane, b_ax, shift(b_ax, 1, 1))
            above = shift(f - q[v], -1, 0)[:rows]
            below = shift(f + q[v], 1, 0)[:rows]
            out.append((left - right) + (below - above) - 4.0 * qc)
        return out

    def wait_halo(side, j):
        dst = qx.at[pl.ds(j * per, per), :, pl.ds(rows if side else ext - 1, 1), :]
        pltpu.make_async_copy(state.at[:, :, pl.ds(0, 1), :], dst, rcv_h.at[side, j]).wait()

    for off in range(n_i):
        j = flip(me, off)
        if off == 0:
            own_copy.wait()
        else:
            pltpu.make_async_copy(
                state.at[:, :, pl.ds(0, rows), :], qx.at[pl.ds(j * per, per), :, pl.ds(0, rows), :],
                rcv_m.at[off]).wait()
        wait_halo(0, j)
        wait_halo(1, j)

        @pl.loop(0, per)
        def _(k, j=j):
            n = j * per + k
            part = flux_part(qx, n)
            for v in range(NV):
                fx[n, v, pl.ds(0, rows), :] = qx[n, v, pl.ds(0, rows), :] + (0.5 * TIME_STEP) * part[v]

    def spectral_first(t):
        @pl.loop(0, NV)
        def _(v):
            sp = spectral([qx[n, v, pl.ds(8 * t, 8), :] for n in range(inst)])
            for n in range(inst):
                fx[n, v, pl.ds(8 * t, 8), :] += (-0.5 * TIME_STEP * FREQUENCY) * sp[n]

    def spectral_last(t):
        @pl.loop(0, NV)
        def _(v):
            sp = spectral([fx[n, v, pl.ds(8 * t, 8), :] for n in range(inst)])
            for n in range(inst):
                rs[n, v, pl.ds(8 * t, 8), :] = -FREQUENCY * sp[n]

    tiles = rows // 8
    edge = sorted({0, tiles - 1})
    inner = [t for t in range(tiles) if t not in edge]
    for t in edge:
        spectral_first(t)

    above_dev = dev(jnp.where(me == n_i - 1, up_w, w), lax.rem(me + 1, n_i))
    below_dev = dev(jnp.where(me == 0, dn_w, w), lax.rem(me + n_i - 1, n_i))
    to_above = pltpu.make_async_remote_copy(
        fx.at[:, :, pl.ds(rows - 1, 1), :], fx.at[:, :, pl.ds(ext - 1, 1), :],
        snd_f.at[0], rcv_f.at[0], device_id=above_dev, device_id_type=MESH)
    to_below = pltpu.make_async_remote_copy(
        fx.at[:, :, pl.ds(0, 1), :], fx.at[:, :, pl.ds(rows, 1), :],
        snd_f.at[1], rcv_f.at[1], device_id=below_dev, device_id_type=MESH)
    to_above.start()
    to_below.start()
    for t in inner:
        spectral_first(t)
    for t in range(tiles):
        spectral_last(t)
    to_above.wait_recv()
    to_below.wait_recv()

    def back(off):
        to = flip(me, off)
        return pltpu.make_async_remote_copy(
            rs.at[pl.ds(to * per, per)], res.at[:, :, pl.ds(me * rows, rows), :],
            snd_r.at[off], rcv_r.at[off], device_id=dev(w, to), device_id_type=MESH)

    own_back = pltpu.make_async_copy(rs.at[mine], res.at[:, :, pl.ds(me * rows, rows), :], own_sem.at[1])
    for off in order_out + [0]:
        j = flip(me, off)

        @pl.loop(0, per)
        def _(k, j=j):
            n = j * per + k
            part = flux_part(fx, n)
            for v in range(NV):
                rs[n, v] += part[v]

        if off == 0:
            own_back.start()
        else:
            back(off).start()

    own_back.wait()
    for off in range(1, n_i):
        main(off).wait_send()
    for side in range(2):
        for i in range(n_i):
            far, remote, local = halo(side, i)
            if far:
                remote.wait_send()
            else:
                @pl.when(me != i)
                def _(remote=remote):
                    remote.wait_send()
    to_above.wait_send()
    to_below.wait_send()
    for off in order_out:
        j = flip(me, off)
        back(off).wait_send()
        pltpu.make_async_copy(rs.at[mine], res.at[:, :, pl.ds(j * rows, rows), :], rcv_r.at[off]).wait()


def body(n_i, n_w, state, slot_blade, blade_class, face_index, amp, phase):
    per, nv, ct, cx = state.shape
    rows = ct // n_i
    inst = per * n_i
    smem = pl.BlockSpec(memory_space=pltpu.SMEM)
    dma = pltpu.SemaphoreType.DMA
    last = pl.pallas_call(
        functools.partial(kernel, n_i, n_w, per, rows),
        out_shape=jax.ShapeDtypeStruct(state.shape, jnp.float32),
        in_specs=[pl.BlockSpec(memory_space=pl.ANY), smem, smem, smem, smem,
                  pl.BlockSpec(memory_space=pltpu.VMEM)],
        out_specs=pl.BlockSpec(memory_space=pl.ANY),
        scratch_shapes=[
            pltpu.VMEM((inst, nv, rows + 8, cx), jnp.float32),
            pltpu.VMEM((inst, nv, rows + 8, cx), jnp.float32),
            pltpu.VMEM((inst, nv, rows, cx), jnp.float32),
            pltpu.VMEM((inst, cx), jnp.float32),
            dma((2,)),
            dma((n_i,)), dma((n_i,)),
            dma((2, n_i)), dma((2, n_i)),
            dma((2,)), dma((2,)),
            dma((n_i,)), dma((n_i,)),
        ],
        compiler_params=pltpu.CompilerParams(
            collective_id=0, has_side_effects=True, vmem_limit_bytes=48 * 1024 * 1024),
        cost_estimate=pl.CostEstimate(flops=50_000_000, bytes_accessed=2_700_000, transcendentals=0),
    )(state, slot_blade, blade_class, amp, phase, face_index)
    return state + TIME_STEP * last, last


def solution(mesh):
    placed = (
        P("inst", None, ("cases", "wheel"), None),
        P(("cases", "wheel")),
        P("cases"),
        P(("cases", "wheel"), None, None),
        P(),
        P(),
    )
    return jax.shard_map(
        functools.partial(body, mesh.shape["inst"], mesh.shape["wheel"]),
        mesh=mesh,
        in_specs=placed,
        out_specs=(
            P("inst", None, ("cases", "wheel"), None),
            P("inst", None, ("cases", "wheel"), None),
        ),
        check_vma=False,
    )
```

time: 128 us -> 49.3 us (0.39)
  waiting for transfers between devices: 43.9 us -> 0 us
  Pallas kernels: 0 us -> 41.5 us
  matrix products: 23.7 us -> 0 us
  other arithmetic: 19.8 us -> 1.22 us
  between operations: 15.1 us -> 1.3 us
  local copies, waits for them, and re-layouts: 15.9 us -> 5.01 us
  starting transfers between devices: 9.12 us -> 0 us
    all_gather x2 -> x0, waiting for transfers between devices: 43.2 us -> none  [spectral_of(): lax.all_gather(field, 'inst', axis=0, tiled=True)]
    pallas_call x0 -> x1, Pallas kernels: none -> 41.5 us  [body(): pl.pallas_call(functools.partial(kernel, n_i, n_w, per, rows), out_shape=...]
    dot_general x2 -> x0, matrix products: 23.7 us -> none  [spectral_of(): jnp.einsum('nm,mvjk->nvjk', own_rows, lax.all_gather(field, 'inst', axis=...]
    sub x5 -> x0, other arithmetic: 12.4 us -> none  [the longest x4 12.4 us: face_terms(): 0.5 * (flux_left + flux_right) - speed * 0.5 * (left + right)]
    ppermute x4 -> x0, starting transfers between devices: 9.04 us -> none  [the longest x2 4.62 us: padded_2(): before = lax.ppermute(last, axis, up)]
    slice x8 -> x0, local copies, waits for them, and re-layouts: 7.13 us -> none  [the longest x2 4.51 us: local_residual(): field[..., :1]]
    gather x8 -> x0, local copies, waits for them, and re-layouts: 3.4 us -> none  [the longest x4 1.7 us: residual_of(): upper = jnp.take(padded[:, :, -1, :], face_row[1], axis=2)]
    reduce_sum x3 -> x0, other arithmetic: 3.21 us -> none  [the longest x1 1.32 us: body(): amplitude = jnp.sum(jnp.where(class_pick, class_amplitude, 0.0))]
  transfers between devices with their start and end apart: 6 -> 0, of which waited for: 2 -> 0; matrix products, arithmetic and copies ran while one was open for 25% -> 0% of each run, Pallas kernels for 0% -> 0%
where the time goes in v1:
time: 49.3 us; the launch traced here: 49.1 us
  Pallas kernels  41.5 us (84%)
  local copies, waits for them, and re-layouts  5.01 us (10%)
  between operations  1.3 us (3%)
  other arithmetic  1.22 us (2%)
    pallas_call x1, Pallas kernels, body(): pl.pallas_call(functools.partial(kernel, n_i, n_w, per, rows), out_shape=...  41.5 us
    unnamed x11, local copies, waits for them, and re-layouts  5.01 us
    add x1, other arithmetic, body(): return (state + TIME_STEP * last, last)  1.22 us

profile of v1, /device:TPU:0, one launch (start us, length us, event | category | flops | bytes accessed | tf_op | source)
XLA Modules:
  0.0 49.1 jit_solution(2146882738945857396)
XLA Ops:
  1.3 0.0 copy-start
  1.3 1.3 %copy-done = f32[4,5,128,128]{3,2,1,0:T(8,128)S(1)} copy-done((f32[4,5,128,128]{3,2,1,0:T(8,128)S(1)}, f32[4,5,128,128]{3,2,1,0:T(8,128)}, u32[]{:S(2)}) %copy-start) | copy-done | bytes 1310744
  2.6 0.0 copy-start.1
  2.6 0.7 %copy-done.1 = s32[1,2,128]{2,1,0:T(2,128)S(1)} copy-done((s32[1,2,128]{2,1,0:T(2,128)S(1)}, s32[1,2,128]{2,1,0:T(2,128)}, u32[]{:S(2)}) %copy-start.1) | copy-done | bytes 1048
  3.3 0.0 copy-start.2
  3.3 0.7 %copy-done.2 = s32[4]{0:T(128)S(1)} copy-done((s32[4]{0:T(128)S(1)}, s32[4]{0:T(128)}, u32[]{:S(2)}) %copy-start.2) | copy-done | bytes 40
  3.9 0.0 copy-start.3
  3.9 0.7 %copy-done.3 = f32[4]{0:T(128)S(1)} copy-done((f32[4]{0:T(128)S(1)}, f32[4]{0:T(128)}, u32[]{:S(2)}) %copy-start.3) | copy-done | bytes 40
  4.6 0.0 copy-start.4
  4.6 0.7 %copy-done.4 = f32[4]{0:T(128)S(1)} copy-done((f32[4]{0:T(128)S(1)}, f32[4]{0:T(128)}, u32[]{:S(2)}) %copy-start.4) | copy-done | bytes 40
  5.2 41.5 %shard_map.77 = f32[4,5,128,128]{3,2,1,0:T(8,128)S(1)} custom-call(f32[4,5,128,128]{3,2,1,0:T(8,128)S(1)} %copy-done, s32[1]{0:T(128)S(6)} %copy.9.slot_blade, s32[4]{0:T(128)S(1)} %copy-done.2, f32[4]{0:T(128)S(1)} %copy-done.3, f32[4]{0:T(128)S(1)} %copy-done.4, s32[1,2,128]{2,1,0:T(2,128)S(1)} %copy-done.1), custom_call_target="tpu_custom_call" | custom-call | flops 50000000 | bytes 2700000 | tf_op jit(solution)/shard_map/pallas_call | solution.py:297
  46.8 1.2 %multiply_add_fusion = f32[4,5,128,128]{3,2,1,0:T(8,128)} fusion(f32[4,5,128,128]{3,2,1,0:T(8,128)S(1)} %copy-done, f32[4,5,128,128]{3,2,1,0:T(8,128)S(1)} %shard_map.77), kind=kLoop, calls=%fused_computation | loop fusion | flops 655360 | bytes 3932160 | tf_op jit(solution)/shard_map/add | solution.py:318
  48.0 1.1 %copy.10 = f32[4,5,128,128]{3,2,1,0:T(8,128)} copy(f32[4,5,128,128]{3,2,1,0:T(8,128)S(1)} %shard_map.77) | data formatting | bytes 2621440
Async XLA Ops:
  1.3 1.3 %copy-start = (f32[4,5,128,128]{3,2,1,0:T(8,128)S(1)}, f32[4,5,128,128]{3,2,1,0:T(8,128)}, u32[]{:S(2)}) copy-start(f32[4,5,128,128]{3,2,1,0:T(8,128)} %state.1) | copy-start | bytes 3932164
  2.6 0.7 %copy-start.1 = (s32[1,2,128]{2,1,0:T(2,128)S(1)}, s32[1,2,128]{2,1,0:T(2,128)}, u32[]{:S(2)}) copy-start(s32[1,2,128]{2,1,0:T(2,128)} %face.1) | copy-start | bytes 3076
  3.3 0.7 %copy-start.2 = (s32[4]{0:T(128)S(1)}, s32[4]{0:T(128)}, u32[]{:S(2)}) copy-start(s32[4]{0:T(128)} %blade_class.1) | copy-start | bytes 52
  3.9 0.7 %copy-start.3 = (f32[4]{0:T(128)S(1)}, f32[4]{0:T(128)}, u32[]{:S(2)}) copy-start(f32[4]{0:T(128)} %amp.1) | copy-start | bytes 52
  4.6 0.7 %copy-start.4 = (f32[4]{0:T(128)S(1)}, f32[4]{0:T(128)}, u32[]{:S(2)}) copy-start(f32[4]{0:T(128)} %phase.1) | copy-start | bytes 52

commit v2 on v1

v2 whole, which is shorter than its diff:
```python
import functools
import math

import jax
import jax.numpy as jnp
from jax import lax
from jax.experimental import pallas as pl
from jax.experimental.pallas import tpu as pltpu
from jax.sharding import PartitionSpec as P

TIME_STEP = 0.05
GAMMA1 = 0.4
FREQUENCY = 0.5
NV = 5
MESH = pl.DeviceIdType.MESH


def flip(i, off):
    out, b = i, 1
    while b <= off:
        if off & b:
            out = out + b - 2 * b * ((i // b) % 2)
        b *= 2
    return out


def spectral(q):
    s = [q[i] + q[i + 8] for i in range(8)]
    d = [q[i] - q[i + 8] for i in range(8)]
    c = [0.5 * (-1) ** k / math.tan(math.pi * k / 8) for k in range(1, 4)]
    t = [0.5 * (-1) ** k / math.sin(math.pi * k / 8) for k in range(1, 4)]
    s2 = [s[i] - s[(i + 2) % 8] for i in range(8)]
    s4 = [s[i] - s[i + 4] for i in range(4)]

    def dd(i):
        i %= 16
        return (d[i], 1) if i < 8 else (d[i - 8], -1)

    cache = {}

    def ddiff(i, j):
        (x, sx), (y, sy) = dd(i), dd(j)
        key = (i % 8, j % 8, sx * sy)
        if key not in cache:
            cache[key] = x - y if sx * sy > 0 else x + y
        return cache[key], sx

    out = [None] * 16
    for n in range(8):
        a1 = s2[(n - 1) % 8]
        a3 = s2[(n + 3) % 8]
        i = (n - 2) % 8
        a2 = s4[i] * c[1] if i < 4 else s4[i - 4] * (-c[1])
        u = c[0] * a1 - c[2] * a3 + a2
        w = None
        for k in (1, 2, 3):
            v, sg = ddiff(n - k, n + k)
            term = v * (sg * t[k - 1])
            w = term if w is None else w + term
        x, sg = dd(n - 4)
        w = w + x * (0.5 * sg)
        out[n] = u + w
        out[n + 8] = u - w
    return out


def shift(x, k, axis):
    size = x.shape[axis]
    return pltpu.roll(x, k % size, axis)


def kernel(n_i, n_w, per, rows, state, slot_blade_h, blade_class_h, amp_h, phase_h, face_h, new, res,
           st, qx, fx, eb, rs, spd, slot_blade, blade_class, amp, phase, face, par_sem, own_sem,
           snd_m, rcv_m, snd_h, rcv_h, snd_f, rcv_f, snd_r, rcv_r):
    me = lax.axis_index("inst")
    w = lax.axis_index("wheel")
    up_w, dn_w = lax.rem(w + 1, n_w), lax.rem(w + n_w - 1, n_w)
    ct = rows * n_i
    inst = n_i * per
    tiles = rows // 8
    arrivals = [0] + ([tiles - 1] if tiles > 1 else []) + list(range(1, tiles - 1))

    def dev(wheel, i):
        return {"wheel": wheel, "inst": i}

    small = [(slot_blade_h, slot_blade), (blade_class_h, blade_class), (amp_h, amp), (phase_h, phase), (face_h, face)]
    for i, (a, b) in enumerate(small):
        pltpu.make_async_copy(a, b, par_sem.at[i]).start()

    barrier = pltpu.get_barrier_semaphore()
    for off in range(1, n_i):
        pl.semaphore_signal(barrier, inc=1, device_id=dev(w, flip(me, off)), device_id_type=MESH)

    @pl.when(me == 0)
    def _():
        for j in range(n_i):
            pl.semaphore_signal(barrier, inc=1, device_id=dev(dn_w, j), device_id_type=MESH)

    @pl.when(me == n_i - 1)
    def _():
        for j in range(n_i):
            pl.semaphore_signal(barrier, inc=1, device_id=dev(up_w, j), device_id_type=MESH)

    mine = pl.ds(me * per, per)
    own_copy = pltpu.make_async_copy(
        state.at[:, :, pl.ds(me * rows, rows), :], qx.at[mine, :, pl.ds(0, rows), :], own_sem.at[0])
    own_copy.start()
    st_copy = pltpu.make_async_copy(state, st, own_sem.at[1])
    for i, (a, b) in enumerate(small):
        pltpu.make_async_copy(a, b, par_sem.at[i]).wait()
    cls = blade_class[slot_blade[0]]
    instance = lax.broadcasted_iota(jnp.int32, (inst, 128), 0).astype(jnp.float32)
    spd[...] = amp[cls] * jnp.sin((2.0 * math.pi / inst) * instance + phase[cls])
    lane = lax.broadcasted_iota(jnp.int32, (8, 128), 1)
    sub = lax.broadcasted_iota(jnp.int32, (8, 128), 0)
    lo_idx = jnp.where(me == 0, face[0, 0:1, :], lane[0:1])
    hi_idx = jnp.where(me == n_i - 1, face[0, 1:2, :], lane[0:1])
    offs = jnp.where(sub == 0, hi_idx, jnp.where(sub == 7, lo_idx, lane)) - lane
    top = sub < 4
    first_lane, last_lane = lane == 0, lane == 127

    pl.semaphore_wait(barrier, n_i + 1)

    def halo(side, i):
        if side == 0:
            row, slot, wheel = (rows * i - 1) % ct, rows + 7, (up_w if i == 0 else w)
            far = i == 0
        else:
            row, slot, wheel = (rows * (i + 1)) % ct, rows, (dn_w if i == n_i - 1 else w)
            far = i == n_i - 1
        src = state.at[:, :, pl.ds(row, 1), :]
        dst = qx.at[mine, :, pl.ds(slot, 1), :]
        remote = pltpu.make_async_remote_copy(
            src, dst, snd_h.at[side, i], rcv_h.at[side, me], device_id=dev(wheel, i), device_id_type=MESH)
        local = pltpu.make_async_copy(src, dst, rcv_h.at[side, me])
        return far, remote, local

    for side in range(2):
        for i in range(n_i):
            far, remote, local = halo(side, i)
            if far:
                remote.start()
            else:
                @pl.when(me != i)
                def _(remote=remote):
                    remote.start()

                @pl.when(me == i)
                def _(local=local):
                    local.start()

    def main(off, t):
        to = flip(me, off)
        return pltpu.make_async_remote_copy(
            state.at[:, :, pl.ds(to * rows + 8 * t, 8), :], qx.at[mine, :, pl.ds(8 * t, 8), :],
            snd_m.at[off, t], rcv_m.at[off, t], device_id=dev(w, to), device_id_type=MESH)

    order_out = list(range(2, n_i)) + [1]
    for t in arrivals:
        for off in order_out:
            main(off, t).start()
    st_copy.start()

    def tile(buf, n, v, t):
        return buf[n, v, pl.ds(8 * t, 8), :]

    def flux_part(n, q, z):
        both = [jnp.concatenate([q[v], z[v]], axis=0) for v in range(NV)]
        rho, mx, mt, mr, en = both
        inv = 1.0 / rho
        ux, ut = mx * inv, mt * inv
        p = GAMMA1 * (en - 0.5 * (mx * ux + mt * ut + mr * mr * inv))
        h = en + p
        hux = 0.5 * ux[:8]
        hut = 0.5 * ut
        hrel = hut - 0.5 * spd[pl.ds(n, 1), :]
        hp = 0.5 * p
        out = []
        for v in range(NV):
            g = (h[:8] if v == 4 else q[v]) * hux
            f = both[v] * hrel
            if v == 1:
                g = g + hp[:8]
            if v == 2:
                f = f + hp
            if v == 4:
                f = f + p * hut
            a_ax, b_ax = g - q[v], g + q[v]
            right = jnp.where(last_lane, a_ax, shift(a_ax, -1, 1))
            left = jnp.where(first_lane, b_ax, shift(b_ax, 1, 1))
            a_pi, b_pi = f - both[v], f + both[v]
            above = shift(jnp.where(sub == 0, a_pi[8:], a_pi[:8]), -1, 0)
            below = shift(jnp.where(sub == 7, b_pi[8:], b_pi[:8]), 1, 0)
            out.append((left - right) + (below - above) - 4.0 * q[v])
        return out

    def around(buf, n, t, above=True):
        hi = t + 1 if above else t
        lo = tiles if t == 0 else t - 1
        return [jnp.where(top, tile(buf, n, v, hi), tile(buf, n, v, lo)) for v in range(NV)]

    def match(buf):
        @pl.loop(0, inst)
        def _(n):
            for v in range(NV):
                x = tile(buf, n, v, tiles)
                buf[n, v, pl.ds(rows, 8), :] = jnp.where(
                    offs == 0, x, jnp.where(offs == 1, shift(x, -1, 1), shift(x, 1, 1)))

    def section_one(t, above=True):
        @pl.loop(0, NV)
        def _(v):
            q = [tile(qx, n, v, t) for n in range(inst)]
            sp = spectral(q)
            for n in range(inst):
                fx[n, v, pl.ds(8 * t, 8), :] = q[n] - (0.5 * TIME_STEP * FREQUENCY) * sp[n]

        @pl.loop(0, inst, unroll=4)
        def _(n):
            part = flux_part(n, [tile(qx, n, v, t) for v in range(NV)], around(qx, n, t, above))
            for v in range(NV):
                fx[n, v, pl.ds(8 * t, 8), :] += (0.5 * TIME_STEP) * part[v]

    def edges_one():
        def pick(n, v):
            return jnp.where(top, tile(qx, n, v, 0), tile(qx, n, v, tiles - 1))

        @pl.loop(0, NV)
        def _(v):
            q = [pick(n, v) for n in range(inst)]
            sp = spectral(q)
            for n in range(inst):
                eb[n, v] = q[n] - (0.5 * TIME_STEP * FREQUENCY) * sp[n]

        @pl.loop(0, inst, unroll=4)
        def _(n):
            part = flux_part(n, [pick(n, v) for v in range(NV)], [tile(qx, n, v, tiles) for v in range(NV)])
            for v in range(NV):
                eb[n, v] += (0.5 * TIME_STEP) * part[v]

    def section_two(t):
        @pl.loop(0, NV)
        def _(v):
            sp = spectral([tile(fx, n, v, t) for n in range(inst)])
            for n in range(inst):
                rs[n, v, pl.ds(8 * t, 8), :] = -FREQUENCY * sp[n]

        @pl.loop(0, inst, unroll=4)
        def _(n):
            part = flux_part(n, [tile(fx, n, v, t) for v in range(NV)], around(fx, n, t))
            for v in range(NV):
                rs[n, v, pl.ds(8 * t, 8), :] += part[v]

    def back(off, t):
        to = flip(me, off)
        return pltpu.make_async_remote_copy(
            rs.at[pl.ds(to * per, per), :, pl.ds(8 * t, 8), :], res.at[:, :, pl.ds(me * rows + 8 * t, 8), :],
            snd_r.at[off, t], rcv_r.at[off, t], device_id=dev(w, to), device_id_type=MESH)

    def arrive(t):
        for off in range(1, n_i):
            pltpu.make_async_copy(
                state.at[:, :, pl.ds(0, 8), :], qx.at[pl.ds(flip(me, off) * per, per), :, pl.ds(8 * t, 8), :],
                rcv_m.at[off, t]).wait()

    to_above = pltpu.make_async_remote_copy(
        eb.at[:, :, pl.ds(7, 1), :], fx.at[:, :, pl.ds(rows + 7, 1), :], snd_f.at[0], rcv_f.at[0],
        device_id=dev(jnp.where(me == n_i - 1, up_w, w), lax.rem(me + 1, n_i)), device_id_type=MESH)
    to_below = pltpu.make_async_remote_copy(
        eb.at[:, :, pl.ds(0, 1), :], fx.at[:, :, pl.ds(rows, 1), :], snd_f.at[1], rcv_f.at[1],
        device_id=dev(jnp.where(me == 0, dn_w, w), lax.rem(me + n_i - 1, n_i)), device_id_type=MESH)

    own_copy.wait()
    for side in range(2):
        for j in range(n_i):
            dst = qx.at[pl.ds(j * per, per), :, pl.ds(rows if side else rows + 7, 1), :]
            pltpu.make_async_copy(state.at[:, :, pl.ds(0, 1), :], dst, rcv_h.at[side, j]).wait()
    match(qx)
    for t in sorted({0, tiles - 1}):
        arrive(t)
    edges_one()
    to_above.start()
    to_below.start()

    def ghosts():
        to_above.wait_recv()
        to_below.wait_recv()
        match(fx)

    def finish(t):
        section_two(t)
        for off in order_out:
            back(off, t).start()

    if tiles > 3:
        arrive(1)
        section_one(0)
        section_one(1, above=False)
        ghosts()
        finish(0)
        for t in range(2, tiles - 1):
            arrive(t)
        for t in range(1, tiles):
            section_one(t)
        rest = range(1, tiles)
    else:
        for t in range(1, tiles - 1):
            arrive(t)
        for t in range(tiles):
            section_one(t)
        ghosts()
        rest = range(tiles)
    for t in rest:
        finish(t)

    st_copy.wait()
    for t in range(tiles):
        for off in [0, 1] + list(range(2, n_i)):
            j = flip(me, off)
            at = pl.ds(pl.multiple_of(j * rows + 8 * t, 8), 8)
            if off:
                pltpu.make_async_copy(
                    rs.at[mine, :, pl.ds(8 * t, 8), :], res.at[:, :, at, :], rcv_r.at[off, t]).wait()

            for k in range(per):
                for v in range(NV):
                    if off:
                        r = res[k, v, at, :]
                    else:
                        r = rs[me * per + k, v, pl.ds(8 * t, 8), :]
                        res[k, v, at, :] = r
                    new[k, v, at, :] = st[k, v, at, :] + TIME_STEP * r

    for t in range(tiles):
        for off in range(1, n_i):
            main(off, t).wait_send()
            back(off, t).wait_send()
    for side in range(2):
        for i in range(n_i):
            far, remote, local = halo(side, i)
            if far:
                remote.wait_send()
            else:
                @pl.when(me != i)
                def _(remote=remote):
                    remote.wait_send()
    to_above.wait_send()
    to_below.wait_send()


def place(new_v, res_v, new, res, sem):
    copies = []
    for k in range(new_v.shape[0]):
        copies.append(pltpu.make_async_copy(new_v.at[k], new.at[k], sem.at[0, k]))
        copies.append(pltpu.make_async_copy(res_v.at[k], res.at[k], sem.at[1, k]))
    for c in copies:
        c.start()
    for c in copies:
        c.wait()


def body(n_i, n_w, state, slot_blade, blade_class, face_index, amp, phase):
    per, nv, ct, cx = state.shape
    rows = ct // n_i
    tiles = rows // 8
    inst = per * n_i
    dma = pltpu.SemaphoreType.DMA
    anywhere = pl.BlockSpec(memory_space=pl.ANY)
    in_vmem = pl.BlockSpec(memory_space=pltpu.VMEM)

    def stay(x):
        return pltpu.with_memory_space_constraint(x, pltpu.HBM)

    new_v, res_v = pl.pallas_call(
        functools.partial(kernel, n_i, n_w, per, rows),
        out_shape=[pltpu.VMEM(state.shape, jnp.float32)] * 2,
        in_specs=[anywhere] * 6,
        out_specs=[in_vmem] * 2,
        scratch_shapes=[
            pltpu.VMEM(state.shape, jnp.float32),
            pltpu.VMEM((inst, nv, rows + 8, cx), jnp.float32),
            pltpu.VMEM((inst, nv, rows + 8, cx), jnp.float32),
            pltpu.VMEM((inst, nv, 8, cx), jnp.float32),
            pltpu.VMEM((inst, nv, rows, cx), jnp.float32),
            pltpu.VMEM((inst, cx), jnp.float32),
            pltpu.SMEM(slot_blade.shape, jnp.int32),
            pltpu.SMEM(blade_class.shape, jnp.int32),
            pltpu.SMEM(amp.shape, jnp.float32),
            pltpu.SMEM(phase.shape, jnp.float32),
            pltpu.VMEM(face_index.shape, jnp.int32),
            dma((5,)),
            dma((2,)),
            dma((n_i, tiles)), dma((n_i, tiles)),
            dma((2, n_i)), dma((2, n_i)),
            dma((2,)), dma((2,)),
            dma((n_i, tiles)), dma((n_i, tiles)),
        ],
        compiler_params=pltpu.CompilerParams(
            collective_id=0, has_side_effects=True, vmem_limit_bytes=32 * 1024 * 1024),
        cost_estimate=pl.CostEstimate(flops=50_000_000, bytes_accessed=2_700_000, transcendentals=0),
    )(stay(state), slot_blade, stay(blade_class), stay(amp), stay(phase), stay(face_index))
    return pl.pallas_call(
        place,
        out_shape=[jax.ShapeDtypeStruct(state.shape, jnp.float32)] * 2,
        in_specs=[anywhere] * 2,
        out_specs=[anywhere] * 2,
        scratch_shapes=[dma((2, per))],
        cost_estimate=pl.CostEstimate(flops=0, bytes_accessed=5_200_000, transcendentals=0),
    )(*[pltpu.with_memory_space_constraint(x, pltpu.VMEM) for x in (new_v, res_v)])


def solution(mesh):
    placed = (
        P("inst", None, ("cases", "wheel"), None),
        P(("cases", "wheel")),
        P("cases"),
        P(("cases", "wheel"), None, None),
        P(),
        P(),
    )
    return jax.shard_map(
        functools.partial(body, mesh.shape["inst"], mesh.shape["wheel"]),
        mesh=mesh,
        in_specs=placed,
        out_specs=(
            P("inst", None, ("cases", "wheel"), None),
            P("inst", None, ("cases", "wheel"), None),
        ),
        check_vma=False,
    )
```

time: 49.3 us -> 43.3 us (0.88)
  local copies, waits for them, and re-layouts: 5.01 us -> 0 us
  other arithmetic: 1.22 us -> 0 us
    unnamed x11 -> x0, local copies, waits for them, and re-layouts: 5.01 us -> none
    pallas_call x0 -> x1, Pallas kernels: none -> 1.55 us  [body(): pl.pallas_call(place, out_shape=[jax.ShapeDtypeStruct(state.shape, jnp.fl...]
    pallas_call x1, Pallas kernels: 41.5 us -> 40 us  [body(): pl.pallas_call(functools.partial(kernel, n_i, n_w, per, rows), out_shape=...]
    add x1 -> x0, other arithmetic: 1.22 us -> none  [body(): return (state + TIME_STEP * last, last)]
where the time goes in v2:
time: 43.3 us; the launch traced here: 42.9 us
  Pallas kernels  41.6 us (96%)
  between operations  1.28 us (3%)
    pallas_call x1, Pallas kernels, body(): pl.pallas_call(functools.partial(kernel, n_i, n_w, per, rows), out_shape=...  40 us
    pallas_call x1, Pallas kernels, body(): pl.pallas_call(place, out_shape=[jax.ShapeDtypeStruct(state.shape, jnp.fl...  1.55 us

profile of v2, /device:TPU:0, one launch (start us, length us, event | category | flops | bytes accessed | tf_op | source)
XLA Modules:
  0.0 42.9 jit_solution(12186518462395366000)
XLA Ops:
  1.3 40.0 %shard_map.77 = (f32[4,5,128,128]{3,2,1,0:T(8,128)S(1)}, f32[4,5,128,128]{3,2,1,0:T(8,128)S(1)}) custom-call(f32[4,5,128,128]{3,2,1,0:T(8,128)} %state.1, s32[1]{0:T(128)S(6)} %copy.8.slot_blade_h, s32[4]{0:T(128)} %blade_class_h.1, f32[4]{0:T(128)} %amp_h.1, f32[4]{0:T(128)} %phase_h.1, s32[1,2,128]{2,1,0:T(2,128)} %face_h.1), custom_call_target="tpu_custom_call" | custom-call | flops 50000000 | bytes 2700000 | tf_op jit(solution)/shard_map/pallas_call | solution.py:374
  41.3 1.5 %shard_map.78 = (f32[4,5,128,128]{3,2,1,0:T(8,128)}, f32[4,5,128,128]{3,2,1,0:T(8,128)}) custom-call(f32[4,5,128,128]{3,2,1,0:T(8,128)S(1)} %get-tuple-element.4.new_v, f32[4,5,128,128]{3,2,1,0:T(8,128)S(1)} %get-tuple-element.5.res_v), custom_call_target="tpu_custom_call" | custom-call | bytes 5200000 | tf_op jit(solution)/shard_map/pallas_call | solution.py:402

commit v3 on v2

--- a/solution.py
+++ b/solution.py
@@ -71,7 +71,7 @@
 
 def kernel(n_i, n_w, per, rows, state, slot_blade_h, blade_class_h, amp_h, phase_h, face_h, new, res,
            st, qx, fx, eb, rs, spd, slot_blade, blade_class, amp, phase, face, par_sem, own_sem,
-           snd_m, rcv_m, snd_h, rcv_h, snd_f, rcv_f, snd_r, rcv_r):
+           joined, around_in, snd_m, rcv_m, snd_h, rcv_h, snd_f, rcv_f, snd_r, rcv_r):
     me = lax.axis_index("inst")
     w = lax.axis_index("wheel")
     up_w, dn_w = lax.rem(w + 1, n_w), lax.rem(w + n_w - 1, n_w)
@@ -88,18 +88,18 @@
         pltpu.make_async_copy(a, b, par_sem.at[i]).start()
 
     barrier = pltpu.get_barrier_semaphore()
-    for off in range(1, n_i):
-        pl.semaphore_signal(barrier, inc=1, device_id=dev(w, flip(me, off)), device_id_type=MESH)
 
     @pl.when(me == 0)
     def _():
-        for j in range(n_i):
-            pl.semaphore_signal(barrier, inc=1, device_id=dev(dn_w, j), device_id_type=MESH)
-
-    @pl.when(me == n_i - 1)
-    def _():
-        for j in range(n_i):
-            pl.semaphore_signal(barrier, inc=1, device_id=dev(up_w, j), device_id_type=MESH)
+        for j in range(1, n_i):
+            pl.semaphore_signal(barrier, inc=1, device_id=dev(w, j), device_id_type=MESH)
+
+    @pl.when(me != 0)
+    def _():
+        for j in range(1, n_i):
+            @pl.when(me != j)
+            def _(j=j):
+                pl.semaphore_signal(barrier, inc=1, device_id=dev(w, j), device_id_type=MESH)
 
     mine = pl.ds(me * per, per)
     own_copy = pltpu.make_async_copy(
@@ -119,7 +119,16 @@
     top = sub < 4
     first_lane, last_lane = lane == 0, lane == 127
 
-    pl.semaphore_wait(barrier, n_i + 1)
+    @pl.when(me != 0)
+    def _():
+        pl.semaphore_wait(barrier, n_i - 1)
+        pl.semaphore_signal(joined, inc=1, device_id=dev(w, 0), device_id_type=MESH)
+
+    @pl.when(me == 0)
+    def _():
+        pl.semaphore_wait(joined, n_i - 1)
+        for other in (up_w, dn_w):
+            pl.semaphore_signal(barrier, inc=1, device_id=dev(other, 0), device_id_type=MESH)
 
     def halo(side, i):
         if side == 0:
@@ -138,9 +147,7 @@
     for side in range(2):
         for i in range(n_i):
             far, remote, local = halo(side, i)
-            if far:
-                remote.start()
-            else:
+            if not far:
                 @pl.when(me != i)
                 def _(remote=remote):
                     remote.start()
@@ -156,7 +163,23 @@
             snd_m.at[off, t], rcv_m.at[off, t], device_id=dev(w, to), device_id_type=MESH)
 
     order_out = list(range(2, n_i)) + [1]
-    for t in arrivals:
+    for t in arrivals[:2]:
+        for off in order_out:
+            main(off, t).start()
+
+    @pl.when(me == 0)
+    def _():
+        pl.semaphore_wait(barrier, 2)
+        for j in range(1, n_i):
+            pl.semaphore_signal(around_in, inc=1, device_id=dev(w, j), device_id_type=MESH)
+
+    @pl.when(me != 0)
+    def _():
+        pl.semaphore_wait(around_in, 1)
+
+    halo(0, 0)[1].start()
+    halo(1, n_i - 1)[1].start()
+    for t in arrivals[2:]:
         for off in order_out:
             main(off, t).start()
     st_copy.start()
@@ -300,9 +323,12 @@
         finish(0)
         for t in range(2, tiles - 1):
             arrive(t)
+        section_one(1)
         for t in range(1, tiles):
-            section_one(t)
-        rest = range(1, tiles)
+            if t + 1 < tiles:
+                section_one(t + 1)
+            finish(t)
+        rest = []
     else:
         for t in range(1, tiles - 1):
             arrive(t)
@@ -390,6 +416,7 @@
             pltpu.VMEM(face_index.shape, jnp.int32),
             dma((5,)),
             dma((2,)),
+            pltpu.SemaphoreType.REGULAR, pltpu.SemaphoreType.REGULAR,
             dma((n_i, tiles)), dma((n_i, tiles)),
             dma((2, n_i)), dma((2, n_i)),
             dma((2,)), dma((2,)),

time: 43.3 us -> 40.9 us (0.945)
  Pallas kernels: 41.6 us -> 39.2 us
    pallas_call x1, Pallas kernels: 40 us -> 37.7 us  [body(): pl.pallas_call(functools.partial(kernel, n_i, n_w, per, rows), out_shape=...]
where the time goes in v3:
time: 40.9 us; the launch traced here: 40.5 us
  Pallas kernels  39.2 us (96%)
  between operations  1.28 us (3%)
    pallas_call x1, Pallas kernels, body(): pl.pallas_call(functools.partial(kernel, n_i, n_w, per, rows), out_shape=...  37.7 us
    pallas_call x1, Pallas kernels, body(): pl.pallas_call(place, out_shape=[jax.ShapeDtypeStruct(state.shape, jnp.fl...  1.55 us

profile of v3, /device:TPU:0, one launch (start us, length us, event | category | flops | bytes accessed | tf_op | source)
XLA Modules:
  0.0 40.5 jit_solution(8937639500079723072)
XLA Ops:
  1.3 37.7 %shard_map.77 = (f32[4,5,128,128]{3,2,1,0:T(8,128)S(1)}, f32[4,5,128,128]{3,2,1,0:T(8,128)S(1)}) custom-call(f32[4,5,128,128]{3,2,1,0:T(8,128)} %state.1, s32[1]{0:T(128)S(6)} %copy.8.slot_blade_h, s32[4]{0:T(128)} %blade_class_h.1, f32[4]{0:T(128)} %amp_h.1, f32[4]{0:T(128)} %phase_h.1, s32[1,2,128]{2,1,0:T(2,128)} %face_h.1), custom_call_target="tpu_custom_call" | custom-call | flops 50000000 | bytes 2700000 | tf_op jit(solution)/shard_map/pallas_call | solution.py:400
  38.9 1.5 %shard_map.78 = (f32[4,5,128,128]{3,2,1,0:T(8,128)}, f32[4,5,128,128]{3,2,1,0:T(8,128)}) custom-call(f32[4,5,128,128]{3,2,1,0:T(8,128)S(1)} %get-tuple-element.4.new_v, f32[4,5,128,128]{3,2,1,0:T(8,128)S(1)} %get-tuple-element.5.res_v), custom_call_target="tpu_custom_call" | custom-call | bytes 5200000 | tf_op jit(solution)/shard_map/pallas_call | solution.py:429

commit v4 on v3

--- a/solution.py
+++ b/solution.py
@@ -70,7 +70,7 @@
 
 
 def kernel(n_i, n_w, per, rows, state, slot_blade_h, blade_class_h, amp_h, phase_h, face_h, new, res,
-           st, qx, fx, eb, rs, spd, slot_blade, blade_class, amp, phase, face, par_sem, own_sem,
+           st, qx, fx, rs, spd, slot_blade, blade_class, amp, phase, face, par_sem, own_sem,
            joined, around_in, snd_m, rcv_m, snd_h, rcv_h, snd_f, rcv_f, snd_r, rcv_r):
     me = lax.axis_index("inst")
     w = lax.axis_index("wheel")
@@ -78,8 +78,6 @@
     ct = rows * n_i
     inst = n_i * per
     tiles = rows // 8
-    arrivals = [0] + ([tiles - 1] if tiles > 1 else []) + list(range(1, tiles - 1))
-
     def dev(wheel, i):
         return {"wheel": wheel, "inst": i}
 
@@ -106,19 +104,6 @@
         state.at[:, :, pl.ds(me * rows, rows), :], qx.at[mine, :, pl.ds(0, rows), :], own_sem.at[0])
     own_copy.start()
     st_copy = pltpu.make_async_copy(state, st, own_sem.at[1])
-    for i, (a, b) in enumerate(small):
-        pltpu.make_async_copy(a, b, par_sem.at[i]).wait()
-    cls = blade_class[slot_blade[0]]
-    instance = lax.broadcasted_iota(jnp.int32, (inst, 128), 0).astype(jnp.float32)
-    spd[...] = amp[cls] * jnp.sin((2.0 * math.pi / inst) * instance + phase[cls])
-    lane = lax.broadcasted_iota(jnp.int32, (8, 128), 1)
-    sub = lax.broadcasted_iota(jnp.int32, (8, 128), 0)
-    lo_idx = jnp.where(me == 0, face[0, 0:1, :], lane[0:1])
-    hi_idx = jnp.where(me == n_i - 1, face[0, 1:2, :], lane[0:1])
-    offs = jnp.where(sub == 0, hi_idx, jnp.where(sub == 7, lo_idx, lane)) - lane
-    top = sub < 4
-    first_lane, last_lane = lane == 0, lane == 127
-
     @pl.when(me != 0)
     def _():
         pl.semaphore_wait(barrier, n_i - 1)
@@ -163,7 +148,7 @@
             snd_m.at[off, t], rcv_m.at[off, t], device_id=dev(w, to), device_id_type=MESH)
 
     order_out = list(range(2, n_i)) + [1]
-    for t in arrivals[:2]:
+    for t in range(min(2, tiles)):
         for off in order_out:
             main(off, t).start()
 
@@ -179,10 +164,23 @@
 
     halo(0, 0)[1].start()
     halo(1, n_i - 1)[1].start()
-    for t in arrivals[2:]:
+    for t in range(2, tiles):
         for off in order_out:
             main(off, t).start()
     st_copy.start()
+
+    for i, (a, b) in enumerate(small):
+        pltpu.make_async_copy(a, b, par_sem.at[i]).wait()
+    cls = blade_class[slot_blade[0]]
+    instance = lax.broadcasted_iota(jnp.int32, (inst, 128), 0).astype(jnp.float32)
+    spd[...] = amp[cls] * jnp.sin((2.0 * math.pi / inst) * instance + phase[cls])
+    lane = lax.broadcasted_iota(jnp.int32, (8, 128), 1)
+    sub = lax.broadcasted_iota(jnp.int32, (8, 128), 0)
+    lo_idx = jnp.where(me == 0, face[0, 0:1, :], lane[0:1])
+    hi_idx = jnp.where(me == n_i - 1, face[0, 1:2, :], lane[0:1])
+    offs = jnp.where(sub == 0, hi_idx, jnp.where(sub == 7, lo_idx, lane)) - lane
+    top = sub < 4
+    first_lane, last_lane = lane == 0, lane == 127
 
     def tile(buf, n, v, t):
         return buf[n, v, pl.ds(8 * t, 8), :]
@@ -223,7 +221,7 @@
         return [jnp.where(top, tile(buf, n, v, hi), tile(buf, n, v, lo)) for v in range(NV)]
 
     def match(buf):
-        @pl.loop(0, inst)
+        @pl.loop(0, inst, unroll=4)
         def _(n):
             for v in range(NV):
                 x = tile(buf, n, v, tiles)
@@ -244,23 +242,6 @@
             for v in range(NV):
                 fx[n, v, pl.ds(8 * t, 8), :] += (0.5 * TIME_STEP) * part[v]
 
-    def edges_one():
-        def pick(n, v):
-            return jnp.where(top, tile(qx, n, v, 0), tile(qx, n, v, tiles - 1))
-
-        @pl.loop(0, NV)
-        def _(v):
-            q = [pick(n, v) for n in range(inst)]
-            sp = spectral(q)
-            for n in range(inst):
-                eb[n, v] = q[n] - (0.5 * TIME_STEP * FREQUENCY) * sp[n]
-
-        @pl.loop(0, inst, unroll=4)
-        def _(n):
-            part = flux_part(n, [pick(n, v) for v in range(NV)], [tile(qx, n, v, tiles) for v in range(NV)])
-            for v in range(NV):
-                eb[n, v] += (0.5 * TIME_STEP) * part[v]
-
     def section_two(t):
         @pl.loop(0, NV)
         def _(v):
@@ -287,10 +268,10 @@
                 rcv_m.at[off, t]).wait()
 
     to_above = pltpu.make_async_remote_copy(
-        eb.at[:, :, pl.ds(7, 1), :], fx.at[:, :, pl.ds(rows + 7, 1), :], snd_f.at[0], rcv_f.at[0],
+        fx.at[:, :, pl.ds(rows - 1, 1), :], fx.at[:, :, pl.ds(rows + 7, 1), :], snd_f.at[0], rcv_f.at[0],
         device_id=dev(jnp.where(me == n_i - 1, up_w, w), lax.rem(me + 1, n_i)), device_id_type=MESH)
     to_below = pltpu.make_async_remote_copy(
-        eb.at[:, :, pl.ds(0, 1), :], fx.at[:, :, pl.ds(rows, 1), :], snd_f.at[1], rcv_f.at[1],
+        fx.at[:, :, pl.ds(0, 1), :], fx.at[:, :, pl.ds(rows, 1), :], snd_f.at[1], rcv_f.at[1],
         device_id=dev(jnp.where(me == 0, dn_w, w), lax.rem(me + n_i - 1, n_i)), device_id_type=MESH)
 
     own_copy.wait()
@@ -299,12 +280,6 @@
             dst = qx.at[pl.ds(j * per, per), :, pl.ds(rows if side else rows + 7, 1), :]
             pltpu.make_async_copy(state.at[:, :, pl.ds(0, 1), :], dst, rcv_h.at[side, j]).wait()
     match(qx)
-    for t in sorted({0, tiles - 1}):
-        arrive(t)
-    edges_one()
-    to_above.start()
-    to_below.start()
-
     def ghosts():
         to_above.wait_recv()
         to_below.wait_recv()
@@ -316,31 +291,39 @@
             back(off, t).start()
 
     if tiles > 3:
+        arrive(0)
         arrive(1)
         section_one(0)
-        section_one(1, above=False)
+        to_below.start()
+        for t in range(1, tiles - 2):
+            arrive(t + 1)
+            section_one(t)
+        section_one(tiles - 2, above=False)
+        for t in range(1, tiles - 2):
+            finish(t)
+        arrive(tiles - 1)
+        section_one(tiles - 1)
+        to_above.start()
+        section_one(tiles - 2)
+        finish(tiles - 2)
         ghosts()
         finish(0)
-        for t in range(2, tiles - 1):
-            arrive(t)
-        section_one(1)
-        for t in range(1, tiles):
-            if t + 1 < tiles:
-                section_one(t + 1)
-            finish(t)
-        rest = []
+        finish(tiles - 1)
+        returns = list(range(1, tiles - 1)) + [0, tiles - 1]
     else:
-        for t in range(1, tiles - 1):
+        for t in range(tiles):
             arrive(t)
         for t in range(tiles):
             section_one(t)
+        to_below.start()
+        to_above.start()
         ghosts()
-        rest = range(tiles)
-    for t in rest:
-        finish(t)
+        for t in range(tiles):
+            finish(t)
+        returns = list(range(tiles))
 
     st_copy.wait()
-    for t in range(tiles):
+    for t in returns:
         for off in [0, 1] + list(range(2, n_i)):
             j = flip(me, off)
             at = pl.ds(pl.multiple_of(j * rows + 8 * t, 8), 8)
@@ -406,7 +389,6 @@
             pltpu.VMEM(state.shape, jnp.float32),
             pltpu.VMEM((inst, nv, rows + 8, cx), jnp.float32),
             pltpu.VMEM((inst, nv, rows + 8, cx), jnp.float32),
-            pltpu.VMEM((inst, nv, 8, cx), jnp.float32),
             pltpu.VMEM((inst, nv, rows, cx), jnp.float32),
             pltpu.VMEM((inst, cx), jnp.float32),
             pltpu.SMEM(slot_blade.shape, jnp.int32),

time: 40.9 us -> 39.3 us (0.961)
  Pallas kernels: 39.2 us -> 37.8 us
    pallas_call x1, Pallas kernels: 37.7 us -> 36.3 us  [body(): pl.pallas_call(functools.partial(kernel, n_i, n_w, per, rows), out_shape=...]
where the time goes in v4:
time: 39.3 us; the launch traced here: 39.1 us
  Pallas kernels  37.8 us (96%)
  between operations  1.28 us (3%)
    pallas_call x1, Pallas kernels, body(): pl.pallas_call(functools.partial(kernel, n_i, n_w, per, rows), out_shape=...  36.3 us
    pallas_call x1, Pallas kernels, body(): pl.pallas_call(place, out_shape=[jax.ShapeDtypeStruct(state.shape, jnp.fl...  1.55 us

profile of v4, /device:TPU:0, one launch (start us, length us, event | category | flops | bytes accessed | tf_op | source)
XLA Modules:
  0.0 39.1 jit_solution(3465793147028115023)
XLA Ops:
  1.3 36.3 %shard_map.77 = (f32[4,5,128,128]{3,2,1,0:T(8,128)S(1)}, f32[4,5,128,128]{3,2,1,0:T(8,128)S(1)}) custom-call(f32[4,5,128,128]{3,2,1,0:T(8,128)} %state.1, s32[1]{0:T(128)S(6)} %copy.8.slot_blade_h, s32[4]{0:T(128)} %blade_class_h.1, f32[4]{0:T(128)} %amp_h.1, f32[4]{0:T(128)} %phase_h.1, s32[1,2,128]{2,1,0:T(2,128)} %face_h.1), custom_call_target="tpu_custom_call" | custom-call | flops 50000000 | bytes 2700000 | tf_op jit(solution)/shard_map/pallas_call | solution.py:383
  37.6 1.5 %shard_map.78 = (f32[4,5,128,128]{3,2,1,0:T(8,128)}, f32[4,5,128,128]{3,2,1,0:T(8,128)}) custom-call(f32[4,5,128,128]{3,2,1,0:T(8,128)S(1)} %get-tuple-element.4.new_v, f32[4,5,128,128]{3,2,1,0:T(8,128)S(1)} %get-tuple-element.5.res_v), custom_call_target="tpu_custom_call" | custom-call | bytes 5200000 | tf_op jit(solution)/shard_map/pallas_call | solution.py:411
